TPU v7x, 32 devices: a whole 2x2x4 slice. The times are simulated.
32 devices in a mesh: qry: 8 (over z, core), lib: 4 (over y, x).
Axes of the slice: x: 2, y: 2, z: 4, core: 2. Of those that a mesh axis runs over, the one named last changes fastest.
Arguments:
- query_prints: bfloat16 [256, 2048], P('qry'), may hold values from -500 to 500, as said below
- library_prints: bfloat16 [24576, 2048], P(('lib', 'qry')), may hold values from -1500 to 1500
- query_atoms: float32 [256, 192], P(('qry', 'lib')), may hold values from -3 to 3, as said below
- conformer_atoms: float32 [24576, 192], P(('lib', 'qry')), may hold values from -3 to 3, as said below
- candidates: int32 [256, 64], P(('qry', 'lib')), may hold values from 0 to 24575, as said below
- candidate_count: int32 [256], P(('qry', 'lib')), may hold values from 16 to 64
- home_row: int32 [24576], replicated, may hold values from 0 to 24575, as said below
Outputs:
- tversky: bfloat16 [256, 24576], P(None, ('lib', 'qry'))
- rescore: float32 [256, 64], P(('qry', 'lib'))
Inputs may be any that keep to these rules, and one draw needn't show every extreme that they name: query_prints rows and columns carry independent positive scales. `query_atoms`: each row holds x, y and z of 48 atom slots, then their weights; a padded slot has weight 0, and every row has at least one atom of positive weight. `conformer_atoms`: each row holds x, y and z of 48 atom slots, then their weights; a padded slot has weight 0, and every row has at least one atom of positive weight. Among the candidates in the rows of one device (8 queries, padding included), at most 36 have storage rows in any one block of rows b * 768 to (b + 1) * 768 - 1; in every draw some such block receives exactly 36 from the rows of every device. `home_row`: a permutation of 0 to 24575.
All inputs are finite; a program needn't handle non-finite values.
Results may differ from a plain program's by a relative error of at most 0.0029.
Values may be sent and summed in bfloat16 or wider, within the bound.
A program may use at most 64 MiB of HBM per device.

v0:
```python
import jax
import jax.numpy as jnp
from jax import lax
from jax.sharding import PartitionSpec as P

SHARPNESS = 0.8
EPSILON = 1e-06


def screen_rows(piece, library):
    scores = lax.dot_general(
        piece, library, (((1,), (1,)), ((), ())), preferred_element_type=jnp.float32
    )
    norms = jnp.sum(jnp.square(piece.astype(jnp.float32)), axis=1, keepdims=True)
    return (scores / (norms + EPSILON)).astype(jnp.bfloat16)


def selector(indices, rows):
    return (jnp.arange(rows, dtype=jnp.int32)[:, None] == indices[None, :]).astype(jnp.float32)


def pick_columns(table, indices):
    picks = selector(indices, table.shape[0])
    columns = lax.dot_general(
        table,
        picks,
        (((0,), (0,)), ((), ())),
        precision=lax.Precision.HIGHEST,
        preferred_element_type=jnp.float32,
    )
    return columns.reshape(4, -1, indices.shape[0])


def pick_rows(table, indices):
    picks = selector(indices, table.shape[0])
    return lax.dot_general(
        picks,
        table,
        (((0,), (0,)), ((), ())),
        precision=lax.Precision.HIGHEST,
        preferred_element_type=jnp.float32,
    )


def to_atoms(flat):
    return flat.reshape(flat.shape[0], 4, -1).transpose(1, 2, 0)


def intersection(first, second):
    dist = jnp.square(first[0][:, None, :] - second[0][None, :, :])
    dist = dist + jnp.square(first[1][:, None, :] - second[1][None, :, :])
    dist = dist + jnp.square(first[2][:, None, :] - second[2][None, :, :])
    return jnp.sum(
        first[3][:, None, :] * second[3][None, :, :] * jnp.exp(-SHARPNESS * dist), axis=(0, 1)
    )


def body(
    query_prints,
    library_prints,
    query_atoms,
    conformer_atoms,
    candidates,
    candidate_count,
    home_row,
):
    query_groups = lax.axis_size("qry")
    library_groups = lax.axis_size("lib")
    devices = query_groups * library_groups
    own_rows = library_prints.shape[0]
    local_queries = query_atoms.shape[0]
    listed = candidates.shape[1]
    pairs = local_queries * listed
    capacity = 2 * ((pairs + devices - 1) // devices) + 4
    tversky = screen_rows(lax.all_gather(query_prints, "qry", axis=0, tiled=True), library_prints)
    stored = jnp.take(home_row, candidates.reshape(-1), axis=0)
    owner = stored // own_rows
    slot_index = stored - owner * own_rows
    first_query = (lax.axis_index("qry") * library_groups + lax.axis_index("lib")) * local_queries
    query_index = first_query + jnp.arange(pairs, dtype=jnp.int32) // listed
    position = jnp.arange(pairs, dtype=jnp.int32)
    earlier = position[:, None] > position[None, :]
    same_owner = owner[:, None] == owner[None, :]
    rank = jnp.sum((earlier & same_owner).astype(jnp.int32), axis=1)
    target = owner * capacity + rank
    bucket_shape = (library_groups, query_groups, capacity)
    send_slot = (
        jnp.zeros(devices * capacity, jnp.int32).at[target].set(slot_index).reshape(bucket_shape)
    )
    send_query = (
        jnp.zeros(devices * capacity, jnp.int32).at[target].set(query_index).reshape(bucket_shape)
    )
    got_slot, got_query = (
        lax.all_to_all(
            lax.all_to_all(send_slot, "qry", split_axis=1, concat_axis=1, tiled=True),
            "lib",
            split_axis=0,
            concat_axis=0,
            tiled=True,
        ),
        lax.all_to_all(
            lax.all_to_all(send_query, "qry", split_axis=1, concat_axis=1, tiled=True),
            "lib",
            split_axis=0,
            concat_axis=0,
            tiled=True,
        ),
    )
    flat_slots = got_slot.reshape(-1)
    fetched = pick_rows(conformer_atoms, flat_slots).reshape(
        library_groups, query_groups, capacity, -1
    )
    prior_all = tversky[got_query.reshape(-1), flat_slots].astype(jnp.float32).reshape(bucket_shape)
    back_atoms, back_prior = (
        lax.all_to_all(
            lax.all_to_all(
                fetched.astype(jnp.bfloat16), "qry", split_axis=1, concat_axis=1, tiled=True
            ),
            "lib",
            split_axis=0,
            concat_axis=0,
            tiled=True,
        ).astype(fetched.dtype),
        lax.all_to_all(
            lax.all_to_all(
                prior_all.astype(jnp.bfloat16), "qry", split_axis=1, concat_axis=1, tiled=True
            ),
            "lib",
            split_axis=0,
            concat_axis=0,
            tiled=True,
        ).astype(prior_all.dtype),
    )
    conformer = pick_columns(back_atoms.reshape(devices * capacity, -1), target)
    fragment = jnp.repeat(to_atoms(query_atoms), listed, axis=2)
    pair_cross = intersection(fragment, conformer)
    pair_self = intersection(conformer, conformer)
    pair_prior = back_prior.reshape(-1)[target]
    own_atoms = to_atoms(query_atoms)
    query_self = jnp.repeat(intersection(own_atoms, own_atoms), listed)
    shape = pair_cross / (query_self + pair_self - pair_cross)
    live = jnp.arange(listed, dtype=jnp.int32)[None, :] < candidate_count[:, None]
    rescore = jnp.where(live, (shape + pair_prior).reshape(local_queries, listed), 0.0)
    return (tversky, rescore)


def solution(mesh):
    return jax.shard_map(
        body,
        mesh=mesh,
        in_specs=(
            P("qry", None),
            P(("lib", "qry"), None),
            P(("qry", "lib"), None),
            P(("lib", "qry"), None),
            P(("qry", "lib"), None),
            P(("qry", "lib")),
            P(),
        ),
        out_specs=(P(None, ("lib", "qry")), P(("qry", "lib"), None)),
        check_vma=False,
    )
```

profile of v0, /device:TPU:0, one launch (start us, length us, event | category | flops | bytes accessed | tf_op | source)
XLA Modules:
  0.0 148.4 jit_solution(1439643963473406378)
XLA Ops:
  7.2 0.9 reshape.300
  8.1 0.8 reshape.301
  8.9 3.6 %gather_fusion = s32[512]{0:T(512)S(1)} fusion(s32[24576]{0:T(1024)} %param.13, s32[1024]{0:T(1024)S(1)} %pad_clamp_fusion.1), kind=kCustom, calls=%fused_computation | custom fusion | bytes 6144 | tf_op jit(solution)/shard_map/jit(_take)/gather | solution.py:76
  12.5 0.3 convert_reduce_fusion
  12.8 2.5 %scatter_custom_fusion = s32[1152]{0:T(1024)S(1)} fusion(s32[512]{0:T(512)S(1)} %bitcast.37, s32[512]{0:T(512)S(1)} %get-tuple-element.4, s32[]{:T(128)} %constant.31.clone.1), kind=kCustom, calls=%fused_computation.44 | custom fusion | bytes 4612 | tf_op jit(solution)/shard_map/scatter | solution.py:88
  15.3 0.1 reshape.302
  15.4 0.7 reshape.354
  16.1 6.3 %all-to-all-start = ((s32[8,1,144]{2,1,0:T(1,128)}), s32[8,1,144]{2,1,0:T(1,128)S(1)}, u32[]{:S(2)}, u32[]{:S(2)}) async-start(s32[8,1,144]{2,1,0:T(1,128)} %reshape.354), calls=%async_computation | async-start | bytes 16384 | tf_op jit(solution)/shard_map/all_to_all | solution.py:95
  22.4 0.7 all-gather.2.cloned.1.call-update
  23.1 4.9 %all-to-all-done = s32[8,1,144]{2,1,0:T(1,128)S(1)} async-done(((s32[8,1,144]{2,1,0:T(1,128)}), s32[8,1,144]{2,1,0:T(1,128)S(1)}, u32[]{:S(2)}, u32[]{:S(2)}) %all-to-all-start) | async-done | bytes 4640 | tf_op jit(solution)/shard_map/all_to_all | solution.py:95
  28.0 0.5 broadcast.324
  28.5 0.7 reduce.2
  29.3 0.7 reshape.356
  29.9 3.7 %all-to-all-start.1 = ((s32[4,1,288]{2,1,0:T(1,128)}), s32[4,1,288]{2,1,0:T(1,128)S(1)}, u32[]{:S(2)}, u32[]{:S(2)}) async-start(s32[4,1,288]{2,1,0:T(1,128)} %reshape.356), calls=%async_computation.1 | async-start | bytes 12288 | tf_op jit(solution)/shard_map/all_to_all | solution.py:94
  33.7 2.4 %scatter_custom_fusion.1 = s32[1152]{0:T(1024)S(1)} fusion(s32[512]{0:T(512)S(1)} %bitcast.38, s32[512]{0:T(512)S(1)} %fusion.19, s32[]{:T(128)} %constant.31.clone.1), kind=kCustom, calls=%fused_computation.42 | custom fusion | bytes 4612 | tf_op jit(solution)/shard_map/scatter | solution.py:91
  36.1 0.1 reshape.304
  36.2 0.7 reshape.358
  36.9 1.4 all-to-all-done.1
  38.3 3.3 %all-to-all-start.4 = ((s32[8,1,144]{2,1,0:T(1,128)}), s32[8,1,144]{2,1,0:T(1,128)S(1)}, u32[]{:S(2)}, u32[]{:S(2)}) async-start(s32[8,1,144]{2,1,0:T(1,128)} %reshape.358), calls=%async_computation.4 | async-start | bytes 16384 | tf_op jit(solution)/shard_map/all_to_all | solution.py:102
  41.7 0.7 reduce.3
  42.4 0.1 eq.45
  42.6 3.4 %fusion.1 = bf16[1152,192]{0,1:T(8,128)(2,1)} fusion(f32[768,192]{0,1:T(8,128)} %param.10, s32[1152]{0:T(1024)S(1)} %eq.45), kind=kOutput, calls=%fused_computation.9 | convolution fusion | flops 2039537664 | bytes 1036800 | tf_op jit(solution)/shard_map/dot_general | solution.py:36
  46.0 2.1 %copy.98 = bf16[1152,192]{1,0:T(8,128)(2,1)} copy(bf16[1152,192]{0,1:T(8,128)(2,1)} %fusion.1) | data formatting | bytes 884736 | tf_op jit(solution)/shard_map/convert_element_type | solution.py:117
  48.0 2.1 %convert_element_type.26 = bf16[4,8,36,192]{3,2,1,0:T(8,128)(2,1)} reshape(bf16[1152,192]{1,0:T(8,128)(2,1)} %copy.98) | data formatting | bytes 884736 | tf_op jit(solution)/shard_map/convert_element_type | solution.py:117
  50.2 2.4 %copy.99 = bf16[4,8,36,192]{3,0,2,1:T(4,128)(2,1)} copy(bf16[4,8,36,192]{3,2,1,0:T(8,128)(2,1)} %convert_element_type.26) | data formatting | bytes 884736 | tf_op jit(solution)/shard_map/convert_element_type | solution.py:117
  52.5 5.0 %all-to-all-start.2 = ((bf16[4,8,36,192]{3,0,2,1:T(4,128)(2,1)}), bf16[4,8,36,192]{3,0,2,1:T(4,128)(2,1)}, u32[]{:S(2)}, u32[]{:S(2)}) async-start(bf16[4,8,36,192]{3,0,2,1:T(4,128)(2,1)} %copy.99), calls=%async_computation.2 | async-start | bytes 1179648 | tf_op jit(solution)/shard_map/all_to_all | solution.py:116
  58.0 0.9 multiply_reduce_fusion.3
  58.9 0.7 reduce.4
  59.7 0.7 reshape.360
  60.4 14.1 %all-to-all-done.2 = bf16[4,8,36,192]{3,0,2,1:T(4,128)(2,1)} async-done(((bf16[4,8,36,192]{3,0,2,1:T(4,128)(2,1)}), bf16[4,8,36,192]{3,0,2,1:T(4,128)(2,1)}, u32[]{:S(2)}, u32[]{:S(2)}) %all-to-all-start.2) | async-done | bytes 442400 | tf_op jit(solution)/shard_map/all_to_all | solution.py:116
  74.4 3.2 %all-to-all-start.5 = ((s32[4,1,288]{2,1,0:T(1,128)}), s32[4,1,288]{2,1,0:T(1,128)S(1)}, u32[]{:S(2)}, u32[]{:S(2)}) async-start(s32[4,1,288]{2,1,0:T(1,128)} %reshape.360), calls=%async_computation.5 | async-start | bytes 12288 | tf_op jit(solution)/shard_map/all_to_all | solution.py:101
  77.7 0.6 pad_clamp_fusion
  78.3 0.1 broadcast_in_dim.47
  78.4 0.7 broadcast_in_dim.48
  79.1 0.1 broadcast_in_dim.51
  79.2 0.7 broadcast_in_dim.52
  80.0 0.1 broadcast_in_dim.53
  80.1 0.7 broadcast_in_dim.54
  80.8 0.1 broadcast_in_dim.55
  81.0 0.7 broadcast_in_dim.56
  81.7 2.1 %copy.100 = bf16[4,8,36,192]{3,1,2,0:T(8,128)(2,1)} copy(bf16[4,8,36,192]{3,0,2,1:T(4,128)(2,1)} %all-to-all-done.2) | data formatting | bytes 884736 | tf_op jit(solution)/shard_map/all_to_all | solution.py:116
  83.8 4.2 %all-to-all-start.3 = ((bf16[4,8,36,192]{3,1,2,0:T(8,128)(2,1)}), bf16[4,8,36,192]{3,1,2,0:T(8,128)(2,1)}, u32[]{:S(2)}, u32[]{:S(2)}) async-start(bf16[4,8,36,192]{3,1,2,0:T(8,128)(2,1)} %copy.100), calls=%async_computation.3 | async-start | bytes 1179648 | tf_op jit(solution)/shard_map/all_to_all | solution.py:115
  88.0 0.1 reshape.306
  88.1 0.7 reduce.5
  88.8 0.1 reshape.305
  89.0 7.8 %all-to-all-done.3 = bf16[4,8,36,192]{3,1,2,0:T(8,128)(2,1)} async-done(((bf16[4,8,36,192]{3,1,2,0:T(8,128)(2,1)}), bf16[4,8,36,192]{3,1,2,0:T(8,128)(2,1)}, u32[]{:S(2)}, u32[]{:S(2)}) %all-to-all-start.3) | async-done | bytes 442400 | tf_op jit(solution)/shard_map/all_to_all | solution.py:115
  96.8 2.0 %copy.101 = bf16[4,8,36,192]{3,2,1,0:T(8,128)(2,1)} copy(bf16[4,8,36,192]{3,1,2,0:T(8,128)(2,1)} %all-to-all-done.3) | data formatting | bytes 884736 | tf_op jit(solution)/shard_map/all_to_all | solution.py:115
  98.8 2.1 %reshape.303 = bf16[1152,192]{1,0:T(8,128)(2,1)} reshape(bf16[4,8,36,192]{3,2,1,0:T(8,128)(2,1)} %copy.101) | data formatting | bytes 884736 | tf_op jit(solution)/shard_map/reshape | solution.py:134
  101.0 2.4 %fusion.2 = f32[192,512]{1,0:T(8,128)} fusion(bf16[1152,192]{1,0:T(8,128)(2,1)} %reshape.303, s32[512]{0:T(512)S(1)} %multiply_add_fusion), kind=kOutput, calls=%fused_computation.11 | convolution fusion | flops 227082240 | bytes 837632 | tf_op jit(solution)/shard_map/dot_general | solution.py:24
  103.4 1.5 %multiply_reduce_fusion.2 = f32[256]{0:T(256)S(1)} fusion(bf16[256,2048]{1,0:T(8,128)(2,1)} %all-gather.2.cloned.1.call-done), kind=kLoop, calls=%fused_computation.12 | loop fusion | flops 1572608 | bytes 1049600 | tf_op jit(solution)/shard_map/reduce_sum | solution.py:14
  104.9 2.2 %fusion.4 = bf16[256,768]{1,0:T(8,128)(2,1)S(1)} fusion(bf16[256,2048]{1,0:T(8,128)(2,1)} %all-gather.2.cloned.1.call-done, bf16[768,2048]{1,0:T(8,128)(2,1)S(1)} %copy-done, f32[256]{0:T(256)S(1)} %broadcast_add_fusion), kind=kOutput, calls=%fused_computation.15 | convolution fusion | flops 805699584 | bytes 4588544 | tf_op jit(solution)/shard_map/dot_general | solution.py:11
  107.2 9.9 %gather_fusion.1 = bf16[1152]{0:T(1024)(128)(2,1)S(1)} fusion(bf16[256,768]{1,0:T(8,128)(2,1)S(1)} %fusion.4, s32[1152]{0:T(1024)S(1)} %fusion.12), kind=kCustom, calls=%fused_computation.1 | custom fusion | bytes 13824 | tf_op jit(solution)/shard_map/gather | solution.py:113
  117.1 0.1 gather.19
  117.2 0.6 copy.111
  117.8 3.3 %all-to-all-start.6 = ((bf16[4,8,36]{2,0,1:T(4,128)(2,1)}), bf16[4,8,36]{2,0,1:T(4,128)(2,1)S(1)}, u32[]{:S(2)}, u32[]{:S(2)}) async-start(bf16[4,8,36]{2,0,1:T(4,128)(2,1)} %copy.111), calls=%async_computation.6 | async-start | bytes 16384 | tf_op jit(solution)/shard_map/all_to_all | solution.py:125
  121.2 1.8 %fusion.24 = (f32[48,512]{1,0:T(8,128)}, f32[48,512]{1,0:T(8,128)}, f32[48,512]{1,0:T(8,128)}, f32[48,512]{1,0:T(8,128)}) fusion(f32[192,512]{1,0:T(8,128)} %fusion.2), kind=kLoop, calls=%fused_computation.60 | loop fusion | bytes 786432 | tf_op jit(solution)/shard_map/slice | solution.py:54
  122.9 3.8 %all-to-all-done.6 = bf16[4,8,36]{2,0,1:T(4,128)(2,1)S(1)} async-done(((bf16[4,8,36]{2,0,1:T(4,128)(2,1)}), bf16[4,8,36]{2,0,1:T(4,128)(2,1)S(1)}, u32[]{:S(2)}, u32[]{:S(2)}) %all-to-all-start.6) | async-done | bytes 2336 | tf_op jit(solution)/shard_map/all_to_all | solution.py:125
  126.7 0.7 reshape.362
  127.4 3.2 %all-to-all-start.7 = ((bf16[4,2,144]{2,1,0:T(2,128)(2,1)}), bf16[4,2,144]{2,1,0:T(2,128)(2,1)S(1)}, u32[]{:S(2)}, u32[]{:S(2)}) async-start(bf16[4,2,144]{2,1,0:T(2,128)(2,1)} %reshape.362), calls=%async_computation.7 | async-start | bytes 8192 | tf_op jit(solution)/shard_map/all_to_all | solution.py:124
  130.6 5.8 %multiply_reduce_fusion = (f32[512]{0:T(512)S(1)}, f32[512]{0:T(512)S(1)}) fusion(f32[48,512]{1,0:T(8,128)} %get-tuple-element.7, f32[48,512]{1,0:T(8,128)} %get-tuple-element.8, f32[48,512]{1,0:T(8,128)} %get-tuple-element.9, f32[48,512]{1,0:T(8,128)} %get-tuple-element.6, f32[48,512]{1,0:T(8,128)} %broadcast_in_dim.56, f32[48,512]{1,0:T(8,128)} %broadcast_in_dim.54, ...), kind=kLoop, calls=%fused_computation.5 | loop fusion | flops 28310528 | bytes 790528 | tf_op jit(solution)/shard_map/reduce_sum | solution.py:53
  136.7 0.1 reshape.363
  136.8 0.1 reshape.310
  136.9 3.3 %gather_fusion.2 = f32[512]{0:T(512)S(1)} fusion(f32[1152]{0:T(1024)S(1)} %reshape.310, s32[1024]{0:T(1024)} %pad_clamp_fusion), kind=kCustom, calls=%fused_computation.2 | custom fusion | bytes 6144 | tf_op jit(solution)/shard_map/gather | solution.py:138
  140.2 1.3 fusion.14
  (39 shorter events, 1.2 us)
Async XLA Ops:
  7.2 97.8 %copy-start = (bf16[768,2048]{1,0:T(8,128)(2,1)S(1)}, bf16[768,2048]{1,0:T(8,128)(2,1)}, u32[]{:S(2)}) copy-start(bf16[768,2048]{1,0:T(8,128)(2,1)} %param.8) | copy-start | bytes 9437188
  16.1 11.9 %all-to-all-start = ((s32[8,1,144]{2,1,0:T(1,128)}), s32[8,1,144]{2,1,0:T(1,128)S(1)}, u32[]{:S(2)}, u32[]{:S(2)}) async-start(s32[8,1,144]{2,1,0:T(1,128)} %reshape.354), calls=%async_computation | async-start | bytes 16384 | tf_op jit(solution)/shard_map/all_to_all | solution.py:95
  22.4 81.0 %all-gather.2.cloned.1.call-start = ((), (), s32[]{:S(2)}) async-start(), calls=%async_computation.8 | async-start | bytes 1179648 | tf_op jit(solution)/shard_map/all_gather | solution.py:75
  29.9 8.4 %all-to-all-start.1 = ((s32[4,1,288]{2,1,0:T(1,128)}), s32[4,1,288]{2,1,0:T(1,128)S(1)}, u32[]{:S(2)}, u32[]{:S(2)}) async-start(s32[4,1,288]{2,1,0:T(1,128)} %reshape.356), calls=%async_computation.1 | async-start | bytes 12288 | tf_op jit(solution)/shard_map/all_to_all | solution.py:94
  38.3 14.2 %all-to-all-start.4 = ((s32[8,1,144]{2,1,0:T(1,128)}), s32[8,1,144]{2,1,0:T(1,128)S(1)}, u32[]{:S(2)}, u32[]{:S(2)}) async-start(s32[8,1,144]{2,1,0:T(1,128)} %reshape.358), calls=%async_computation.4 | async-start | bytes 16384 | tf_op jit(solution)/shard_map/all_to_all | solution.py:102
  42.6 15.0 %copy-start.2 = (f32[8,192]{1,0:T(8,128)S(1)}, f32[8,192]{1,0:T(8,128)}, u32[]{:S(2)}) copy-start(f32[8,192]{1,0:T(8,128)} %param.9) | copy-start | bytes 18436
  52.5 21.9 %all-to-all-start.2 = ((bf16[4,8,36,192]{3,0,2,1:T(4,128)(2,1)}), bf16[4,8,36,192]{3,0,2,1:T(4,128)(2,1)}, u32[]{:S(2)}, u32[]{:S(2)}) async-start(bf16[4,8,36,192]{3,0,2,1:T(4,128)(2,1)} %copy.99), calls=%async_computation.2 | async-start | bytes 1179648 | tf_op jit(solution)/shard_map/all_to_all | solution.py:116
  74.4 9.3 %all-to-all-start.5 = ((s32[4,1,288]{2,1,0:T(1,128)}), s32[4,1,288]{2,1,0:T(1,128)S(1)}, u32[]{:S(2)}, u32[]{:S(2)}) async-start(s32[4,1,288]{2,1,0:T(1,128)} %reshape.360), calls=%async_computation.5 | async-start | bytes 12288 | tf_op jit(solution)/shard_map/all_to_all | solution.py:101
  83.8 13.0 %all-to-all-start.3 = ((bf16[4,8,36,192]{3,1,2,0:T(8,128)(2,1)}), bf16[4,8,36,192]{3,1,2,0:T(8,128)(2,1)}, u32[]{:S(2)}, u32[]{:S(2)}) async-start(bf16[4,8,36,192]{3,1,2,0:T(8,128)(2,1)} %copy.100), calls=%async_computation.3 | async-start | bytes 1179648 | tf_op jit(solution)/shard_map/all_to_all | solution.py:115
  107.2 29.3 %copy-start.1 = (bf16[256,768]{1,0:T(8,128)(2,1)}, bf16[256,768]{1,0:T(8,128)(2,1)S(1)}, u32[]{:S(2)}) copy-start(bf16[256,768]{1,0:T(8,128)(2,1)S(1)} %fusion.4) | copy-start | bytes 1179652
  117.8 8.9 %all-to-all-start.6 = ((bf16[4,8,36]{2,0,1:T(4,128)(2,1)}), bf16[4,8,36]{2,0,1:T(4,128)(2,1)S(1)}, u32[]{:S(2)}, u32[]{:S(2)}) async-start(bf16[4,8,36]{2,0,1:T(4,128)(2,1)} %copy.111), calls=%async_computation.6 | async-start | bytes 16384 | tf_op jit(solution)/shard_map/all_to_all | solution.py:125
  127.4 9.3 %all-to-all-start.7 = ((bf16[4,2,144]{2,1,0:T(2,128)(2,1)}), bf16[4,2,144]{2,1,0:T(2,128)(2,1)S(1)}, u32[]{:S(2)}, u32[]{:S(2)}) async-start(bf16[4,2,144]{2,1,0:T(2,128)(2,1)} %reshape.362), calls=%async_computation.7 | async-start | bytes 8192 | tf_op jit(solution)/shard_map/all_to_all | solution.py:124
  130.6 9.6 %copy-start.3 = (f32[8]{0:T(128)S(1)}, f32[8]{0:T(128)}, u32[]{:S(2)}) copy-start(f32[8]{0:T(128)} %multiply_reduce_fusion.3) | copy-start | bytes 100
Sparse Core Ops, SparseCore 0:
  24.8 23.5 all-gather.1
where the time goes:
time: 150 us; the launch traced here: 148 us
  local copies, waits for them, and re-layouts  47.7 us (32%)
  waiting for transfers between devices  32.6 us (22%)
  starting transfers between devices  32.4 us (22%)
  between operations  14.3 us (10%)
  other arithmetic  13.2 us (9%)
  matrix products  8.09 us (5%)
    all_to_all x1, waiting for transfers between devices, body(): lax.all_to_all(fetched.astype(jnp.bfloat16), 'qry', split_axis=1, concat_...  14.1 us
    gather x3, local copies, waits for them, and re-layouts, body(): tversky[got_query.reshape(-1), flat_slots].astype(jnp.float32)  10.6 us
    all_to_all x1, waiting for transfers between devices, body(): lax.all_to_all(lax.all_to_all(fetched.astype(jnp.bfloat16), 'qry', split_...  7.83 us
    reduce_sum x2, other arithmetic, intersection(): jnp.sum(first[3][:, None, :] * second[3][None, :, :] * jnp.exp(-SHARPNESS...  6.76 us
    convert_element_type x3, local copies, waits for them, and re-layouts, body(): fetched.astype(jnp.bfloat16)  6.56 us
    all_to_all x1, starting transfers between devices, body(): lax.all_to_all(send_slot, 'qry', split_axis=1, concat_axis=1, tiled=True)  6.33 us
    all_to_all x1, starting transfers between devices, body(): lax.all_to_all(fetched.astype(jnp.bfloat16), 'qry', split_axis=1, concat_...  5.03 us
    all_to_all x1, waiting for transfers between devices, body(): lax.all_to_all(send_slot, 'qry', split_axis=1, concat_axis=1, tiled=True)  4.87 us
  transfers between devices with their start and end apart: 9, of which 5 were waited for; matrix products, arithmetic and copies ran while one was open for 27% of the time, Pallas kernels for 0%

commit v1 on v0

--- a/solution.py
+++ b/solution.py
@@ -5,6 +5,13 @@
 
 SHARPNESS = 0.8
 EPSILON = 1e-06
+
+
+def stacked_exchange(array, axis, split, join):
+    size = lax.axis_size(axis)
+    parts = jnp.stack(jnp.split(array, size, axis=split), axis=0)
+    parts = lax.all_to_all(parts, axis, split_axis=0, concat_axis=0)
+    return jnp.concatenate(parts, axis=join)
 
 
 def screen_rows(piece, library):
@@ -113,9 +120,7 @@
     prior_all = tversky[got_query.reshape(-1), flat_slots].astype(jnp.float32).reshape(bucket_shape)
     back_atoms, back_prior = (
         lax.all_to_all(
-            lax.all_to_all(
-                fetched.astype(jnp.bfloat16), "qry", split_axis=1, concat_axis=1, tiled=True
-            ),
+            stacked_exchange(fetched.astype(jnp.bfloat16), "qry", 1, 1),
             "lib",
             split_axis=0,
             concat_axis=0,

time: 150 us -> 156 us (1.040)
  local copies, waits for them, and re-layouts: 47.7 us -> 53.6 us
    unnamed x18 -> x25, local copies, waits for them, and re-layouts: 3.86 us -> 10.1 us
    convert_element_type x3 -> x2, local copies, waits for them, and re-layouts: 6.56 us -> 4.22 us  [body(): fetched.astype(jnp.bfloat16)]
    reshape x0 -> x1, local copies, waits for them, and re-layouts: none -> 2.07 us  [stacked_exchange(): return jnp.concatenate(parts, axis=join)]
    all_to_all x2 -> x1, local copies, waits for them, and re-layouts: 4.11 us -> 2.04 us  [body(): lax.all_to_all(stacked_exchange(fetched.astype(jnp.bfloat16), 'qry', 1, 1...]
    another operation x0 -> x2, local copies, waits for them, and re-layouts: none -> 1.94 us  [stacked_exchange(): parts = jnp.stack(jnp.split(array, size, axis=split), axis=0)]
  transfers between devices with their start and end apart: 9 -> 9, of which waited for: 5 -> 5; matrix products, arithmetic and copies ran while one was open for 27% -> 30% of each run, Pallas kernels for 0% -> 0%
where the time goes in v1:
time: 156 us; the launch traced here: 154 us
  local copies, waits for them, and re-layouts  53.6 us (34%)
  waiting for transfers between devices  32.6 us (21%)
  starting transfers between devices  32.4 us (21%)
  between operations  14.3 us (9%)
  other arithmetic  13.2 us (8%)
  matrix products  8.09 us (5%)
    all_to_all x1, waiting for transfers between devices, stacked_exchange(): parts = lax.all_to_all(parts, axis, split_axis=0, concat_axis=0)  14.1 us
    gather x3, local copies, waits for them, and re-layouts, body(): tversky[got_query.reshape(-1), flat_slots].astype(jnp.float32)  10.6 us
    unnamed x25, local copies, waits for them, and re-layouts  10.1 us
    all_to_all x1, waiting for transfers between devices, body(): lax.all_to_all(stacked_exchange(fetched.astype(jnp.bfloat16), 'qry', 1, 1...  7.83 us
    reduce_sum x2, other arithmetic, intersection(): jnp.sum(first[3][:, None, :] * second[3][None, :, :] * jnp.exp(-SHARPNESS...  6.76 us
    all_to_all x1, starting transfers between devices, body(): lax.all_to_all(send_slot, 'qry', split_axis=1, concat_axis=1, tiled=True)  6.33 us
    all_to_all x1, starting transfers between devices, stacked_exchange(): parts = lax.all_to_all(parts, axis, split_axis=0, concat_axis=0)  5.03 us
    all_to_all x1, waiting for transfers between devices, body(): lax.all_to_all(send_slot, 'qry', split_axis=1, concat_axis=1, tiled=True)  4.87 us
  transfers between devices with their start and end apart: 9, of which 5 were waited for; matrix products, arithmetic and copies ran while one was open for 30% of the time, Pallas kernels for 0%

profile of v1, /device:TPU:0, one launch (start us, length us, event | category | flops | bytes accessed | tf_op | source)
XLA Modules:
  0.0 154.2 jit_solution(11124189556459069272)
XLA Ops:
  7.2 0.9 reshape.306
  8.1 0.8 reshape.307
  8.9 3.6 %gather_fusion = s32[512]{0:T(512)S(1)} fusion(s32[24576]{0:T(1024)} %param.13, s32[1024]{0:T(1024)S(1)} %pad_clamp_fusion.1), kind=kCustom, calls=%fused_computation | custom fusion | bytes 6144 | tf_op jit(solution)/shard_map/jit(_take)/gather | solution.py:83
  12.5 0.3 convert_reduce_fusion
  12.8 2.5 %scatter_custom_fusion = s32[1152]{0:T(1024)S(1)} fusion(s32[512]{0:T(512)S(1)} %bitcast.84, s32[512]{0:T(512)S(1)} %get-tuple-element.4, s32[]{:T(128)} %constant.31.clone.1), kind=kCustom, calls=%fused_computation.60 | custom fusion | bytes 4612 | tf_op jit(solution)/shard_map/scatter | solution.py:95
  15.4 0.7 reshape.362
  16.1 6.3 %all-to-all-start = ((s32[8,1,144]{2,1,0:T(1,128)}), s32[8,1,144]{2,1,0:T(1,128)S(1)}, u32[]{:S(2)}, u32[]{:S(2)}) async-start(s32[8,1,144]{2,1,0:T(1,128)} %reshape.362), calls=%async_computation | async-start | bytes 16384 | tf_op jit(solution)/shard_map/all_to_all | solution.py:102
  22.4 0.7 all-gather.2.cloned.1.call-update
  23.1 4.9 %all-to-all-done = s32[8,1,144]{2,1,0:T(1,128)S(1)} async-done(((s32[8,1,144]{2,1,0:T(1,128)}), s32[8,1,144]{2,1,0:T(1,128)S(1)}, u32[]{:S(2)}, u32[]{:S(2)}) %all-to-all-start) | async-done | bytes 4640 | tf_op jit(solution)/shard_map/all_to_all | solution.py:102
  28.0 0.5 broadcast.324
  28.5 0.7 reduce.2
  29.3 0.7 reshape.364
  29.9 3.7 %all-to-all-start.1 = ((s32[4,1,288]{2,1,0:T(1,128)}), s32[4,1,288]{2,1,0:T(1,128)S(1)}, u32[]{:S(2)}, u32[]{:S(2)}) async-start(s32[4,1,288]{2,1,0:T(1,128)} %reshape.364), calls=%async_computation.1 | async-start | bytes 12288 | tf_op jit(solution)/shard_map/all_to_all | solution.py:101
  33.7 2.4 %scatter_custom_fusion.1 = s32[1152]{0:T(1024)S(1)} fusion(s32[512]{0:T(512)S(1)} %bitcast.85, s32[512]{0:T(512)S(1)} %fusion.27, s32[]{:T(128)} %constant.31.clone.1), kind=kCustom, calls=%fused_computation.58 | custom fusion | bytes 4612 | tf_op jit(solution)/shard_map/scatter | solution.py:98
  36.2 0.7 reshape.366
  36.9 1.4 all-to-all-done.1
  38.3 3.3 %all-to-all-start.4 = ((s32[8,1,144]{2,1,0:T(1,128)}), s32[8,1,144]{2,1,0:T(1,128)S(1)}, u32[]{:S(2)}, u32[]{:S(2)}) async-start(s32[8,1,144]{2,1,0:T(1,128)} %reshape.366), calls=%async_computation.4 | async-start | bytes 16384 | tf_op jit(solution)/shard_map/all_to_all | solution.py:109
  41.7 0.7 reduce.3
  42.6 3.4 %fusion.1 = bf16[1152,192]{0,1:T(8,128)(2,1)} fusion(f32[768,192]{0,1:T(8,128)} %param.10, s32[1152]{0:T(1024)S(1)} %eq.45), kind=kOutput, calls=%fused_computation.9 | convolution fusion | flops 2039537664 | bytes 1036800 | tf_op jit(solution)/shard_map/dot_general | solution.py:43
  46.0 2.1 %copy.138 = bf16[1152,192]{1,0:T(8,128)(2,1)} copy(bf16[1152,192]{0,1:T(8,128)(2,1)} %fusion.1) | data formatting | bytes 884736 | tf_op jit(solution)/shard_map/convert_element_type | solution.py:123
  48.0 2.1 %convert_element_type.26 = bf16[4,8,36,192]{3,2,1,0:T(8,128)(2,1)} reshape(bf16[1152,192]{1,0:T(8,128)(2,1)} %copy.138) | data formatting | bytes 884736 | tf_op jit(solution)/shard_map/convert_element_type | solution.py:123
  50.2 0.9 fusion.14
  51.1 0.9 fusion.13
  52.0 0.9 fusion.12
  52.9 0.9 fusion.11
  53.8 0.9 fusion.10
  54.6 0.9 fusion.9
  55.5 0.9 fusion.8
  56.4 0.9 fusion.7
  57.3 1.0 copy.147
  58.4 5.0 %all-to-all-start.2 = ((bf16[8,4,1,36,192]{4,1,3,2,0:T(4,128)(2,1)}), bf16[8,4,1,36,192]{4,1,3,2,0:T(4,128)(2,1)}, u32[]{:S(2)}, u32[]{:S(2)}) async-start(bf16[8,4,1,36,192]{4,1,3,2,0:T(4,128)(2,1)} %copy.147), calls=%async_computation.2 | async-start | bytes 1179648 | tf_op jit(solution)/shard_map/all_to_all | solution.py:13
  63.8 0.9 multiply_reduce_fusion.3
  64.7 0.7 reduce.4
  65.5 0.7 reshape.368
  66.2 14.1 %all-to-all-done.2 = bf16[8,4,1,36,192]{4,1,3,2,0:T(4,128)(2,1)} async-done(((bf16[8,4,1,36,192]{4,1,3,2,0:T(4,128)(2,1)}), bf16[8,4,1,36,192]{4,1,3,2,0:T(4,128)(2,1)}, u32[]{:S(2)}, u32[]{:S(2)}) %all-to-all-start.2) | async-done | bytes 442400 | tf_op jit(solution)/shard_map/all_to_all | solution.py:13
  80.3 3.2 %all-to-all-start.5 = ((s32[4,1,288]{2,1,0:T(1,128)}), s32[4,1,288]{2,1,0:T(1,128)S(1)}, u32[]{:S(2)}, u32[]{:S(2)}) async-start(s32[4,1,288]{2,1,0:T(1,128)} %reshape.368), calls=%async_computation.5 | async-start | bytes 12288 | tf_op jit(solution)/shard_map/all_to_all | solution.py:108
  83.5 0.6 pad_clamp_fusion
  84.2 0.7 broadcast_in_dim.48
  85.1 0.7 broadcast_in_dim.52
  85.9 0.7 broadcast_in_dim.54
  86.8 0.7 broadcast_in_dim.56
  87.5 2.1 %copy.148 = bf16[4,8,36,192]{3,1,2,0:T(8,128)(2,1)} copy(bf16[4,8,36,192]{3,0,2,1:T(4,128)(2,1)} %bitcast.15) | data formatting | bytes 884736 | tf_op jit(solution)/shard_map/reshape | solution.py:14
  89.6 4.2 %all-to-all-start.3 = ((bf16[4,8,36,192]{3,1,2,0:T(8,128)(2,1)}), bf16[4,8,36,192]{3,1,2,0:T(8,128)(2,1)}, u32[]{:S(2)}, u32[]{:S(2)}) async-start(bf16[4,8,36,192]{3,1,2,0:T(8,128)(2,1)} %copy.148), calls=%async_computation.3 | async-start | bytes 1179648 | tf_op jit(solution)/shard_map/all_to_all | solution.py:122
  93.8 0.1 reshape.314
  93.9 0.7 reduce.5
  94.7 0.1 reshape.313
  94.8 7.8 %all-to-all-done.3 = bf16[4,8,36,192]{3,1,2,0:T(8,128)(2,1)} async-done(((bf16[4,8,36,192]{3,1,2,0:T(8,128)(2,1)}), bf16[4,8,36,192]{3,1,2,0:T(8,128)(2,1)}, u32[]{:S(2)}, u32[]{:S(2)}) %all-to-all-start.3) | async-done | bytes 442400 | tf_op jit(solution)/shard_map/all_to_all | solution.py:122
  102.6 2.0 %copy.149 = bf16[4,8,36,192]{3,2,1,0:T(8,128)(2,1)} copy(bf16[4,8,36,192]{3,1,2,0:T(8,128)(2,1)} %all-to-all-done.3) | data formatting | bytes 884736 | tf_op jit(solution)/shard_map/all_to_all | solution.py:122
  104.7 2.1 %reshape.311 = bf16[1152,192]{1,0:T(8,128)(2,1)} reshape(bf16[4,8,36,192]{3,2,1,0:T(8,128)(2,1)} %copy.149) | data formatting | bytes 884736 | tf_op jit(solution)/shard_map/reshape | solution.py:139
  106.8 2.4 %fusion.2 = f32[192,512]{1,0:T(8,128)} fusion(bf16[1152,192]{1,0:T(8,128)(2,1)} %reshape.311, s32[512]{0:T(512)S(1)} %multiply_add_fusion), kind=kOutput, calls=%fused_computation.11 | convolution fusion | flops 227082240 | bytes 837632 | tf_op jit(solution)/shard_map/dot_general | solution.py:31
  109.2 1.5 multiply_reduce_fusion.2
  110.8 2.2 %fusion.4 = bf16[256,768]{1,0:T(8,128)(2,1)S(1)} fusion(bf16[256,2048]{1,0:T(8,128)(2,1)} %all-gather.2.cloned.1.call-done, bf16[768,2048]{1,0:T(8,128)(2,1)S(1)} %copy-done, f32[256]{0:T(256)S(1)} %broadcast_add_fusion), kind=kOutput, calls=%fused_computation.15 | convolution fusion | flops 805699584 | bytes 4588544 | tf_op jit(solution)/shard_map/dot_general | solution.py:18
  113.0 9.9 %gather_fusion.1 = bf16[1152]{0:T(1024)(128)(2,1)S(1)} fusion(bf16[256,768]{1,0:T(8,128)(2,1)S(1)} %fusion.4, s32[1152]{0:T(1024)S(1)} %fusion.20), kind=kCustom, calls=%fused_computation.1 | custom fusion | bytes 13824 | tf_op jit(solution)/shard_map/gather | solution.py:120
  123.0 0.1 gather.19
  123.1 0.6 copy.159
  123.7 3.3 %all-to-all-start.6 = ((bf16[4,8,36]{2,0,1:T(4,128)(2,1)}), bf16[4,8,36]{2,0,1:T(4,128)(2,1)S(1)}, u32[]{:S(2)}, u32[]{:S(2)}) async-start(bf16[4,8,36]{2,0,1:T(4,128)(2,1)} %copy.159), calls=%async_computation.6 | async-start | bytes 16384 | tf_op jit(solution)/shard_map/all_to_all | solution.py:130
  127.0 1.8 %fusion.32 = (f32[48,512]{1,0:T(8,128)}, f32[48,512]{1,0:T(8,128)}, f32[48,512]{1,0:T(8,128)}, f32[48,512]{1,0:T(8,128)}) fusion(f32[192,512]{1,0:T(8,128)} %fusion.2), kind=kLoop, calls=%fused_computation.76 | loop fusion | bytes 786432 | tf_op jit(solution)/shard_map/slice | solution.py:61
  128.8 3.8 %all-to-all-done.6 = bf16[4,8,36]{2,0,1:T(4,128)(2,1)S(1)} async-done(((bf16[4,8,36]{2,0,1:T(4,128)(2,1)}), bf16[4,8,36]{2,0,1:T(4,128)(2,1)S(1)}, u32[]{:S(2)}, u32[]{:S(2)}) %all-to-all-start.6) | async-done | bytes 2336 | tf_op jit(solution)/shard_map/all_to_all | solution.py:130
  132.5 0.7 reshape.370
  133.2 3.2 %all-to-all-start.7 = ((bf16[4,2,144]{2,1,0:T(2,128)(2,1)}), bf16[4,2,144]{2,1,0:T(2,128)(2,1)S(1)}, u32[]{:S(2)}, u32[]{:S(2)}) async-start(bf16[4,2,144]{2,1,0:T(2,128)(2,1)} %reshape.370), calls=%async_computation.7 | async-start | bytes 8192 | tf_op jit(solution)/shard_map/all_to_all | solution.py:129
  136.5 5.8 %multiply_reduce_fusion = (f32[512]{0:T(512)S(1)}, f32[512]{0:T(512)S(1)}) fusion(f32[48,512]{1,0:T(8,128)} %get-tuple-element.7, f32[48,512]{1,0:T(8,128)} %get-tuple-element.8, f32[48,512]{1,0:T(8,128)} %get-tuple-element.9, f32[48,512]{1,0:T(8,128)} %get-tuple-element.6, f32[48,512]{1,0:T(8,128)} %broadcast_in_dim.56, f32[48,512]{1,0:T(8,128)} %broadcast_in_dim.54, ...), kind=kLoop, calls=%fused_computation.5 | loop fusion | flops 28310528 | bytes 790528 | tf_op jit(solution)/shard_map/reduce_sum | solution.py:60
  142.6 0.1 reshape.318
  142.7 3.3 %gather_fusion.2 = f32[512]{0:T(512)S(1)} fusion(f32[1152]{0:T(1024)S(1)} %reshape.318, s32[1024]{0:T(1024)} %pad_clamp_fusion), kind=kCustom, calls=%fused_computation.2 | custom fusion | bytes 6144 | tf_op jit(solution)/shard_map/gather | solution.py:143
  146.1 1.3 fusion.22
  (47 shorter events, 2.0 us)
Async XLA Ops:
  7.2 103.6 %copy-start = (bf16[768,2048]{1,0:T(8,128)(2,1)S(1)}, bf16[768,2048]{1,0:T(8,128)(2,1)}, u32[]{:S(2)}) copy-start(bf16[768,2048]{1,0:T(8,128)(2,1)} %param.8) | copy-start | bytes 9437188
  16.1 11.9 %all-to-all-start = ((s32[8,1,144]{2,1,0:T(1,128)}), s32[8,1,144]{2,1,0:T(1,128)S(1)}, u32[]{:S(2)}, u32[]{:S(2)}) async-start(s32[8,1,144]{2,1,0:T(1,128)} %reshape.362), calls=%async_computation | async-start | bytes 16384 | tf_op jit(solution)/shard_map/all_to_all | solution.py:102
  22.4 86.9 %all-gather.2.cloned.1.call-start = ((), (), s32[]{:S(2)}) async-start(), calls=%async_computation.8 | async-start | bytes 1179648 | tf_op jit(solution)/shard_map/all_gather | solution.py:82
  29.9 8.4 %all-to-all-start.1 = ((s32[4,1,288]{2,1,0:T(1,128)}), s32[4,1,288]{2,1,0:T(1,128)S(1)}, u32[]{:S(2)}, u32[]{:S(2)}) async-start(s32[4,1,288]{2,1,0:T(1,128)} %reshape.364), calls=%async_computation.1 | async-start | bytes 12288 | tf_op jit(solution)/shard_map/all_to_all | solution.py:101
  38.3 20.0 %all-to-all-start.4 = ((s32[8,1,144]{2,1,0:T(1,128)}), s32[8,1,144]{2,1,0:T(1,128)S(1)}, u32[]{:S(2)}, u32[]{:S(2)}) async-start(s32[8,1,144]{2,1,0:T(1,128)} %reshape.366), calls=%async_computation.4 | async-start | bytes 16384 | tf_op jit(solution)/shard_map/all_to_all | solution.py:109
  46.0 17.5 %copy-start.2 = (f32[8,192]{1,0:T(8,128)S(1)}, f32[8,192]{1,0:T(8,128)}, u32[]{:S(2)}) copy-start(f32[8,192]{1,0:T(8,128)} %param.9) | copy-start | bytes 18436
  58.4 21.9 %all-to-all-start.2 = ((bf16[8,4,1,36,192]{4,1,3,2,0:T(4,128)(2,1)}), bf16[8,4,1,36,192]{4,1,3,2,0:T(4,128)(2,1)}, u32[]{:S(2)}, u32[]{:S(2)}) async-start(bf16[8,4,1,36,192]{4,1,3,2,0:T(4,128)(2,1)} %copy.147), calls=%async_computation.2 | async-start | bytes 1179648 | tf_op jit(solution)/shard_map/all_to_all | solution.py:13
  80.3 9.3 %all-to-all-start.5 = ((s32[4,1,288]{2,1,0:T(1,128)}), s32[4,1,288]{2,1,0:T(1,128)S(1)}, u32[]{:S(2)}, u32[]{:S(2)}) async-start(s32[4,1,288]{2,1,0:T(1,128)} %reshape.368), calls=%async_computation.5 | async-start | bytes 12288 | tf_op jit(solution)/shard_map/all_to_all | solution.py:108
  89.6 13.0 %all-to-all-start.3 = ((bf16[4,8,36,192]{3,1,2,0:T(8,128)(2,1)}), bf16[4,8,36,192]{3,1,2,0:T(8,128)(2,1)}, u32[]{:S(2)}, u32[]{:S(2)}) async-start(bf16[4,8,36,192]{3,1,2,0:T(8,128)(2,1)} %copy.148), calls=%async_computation.3 | async-start | bytes 1179648 | tf_op jit(solution)/shard_map/all_to_all | solution.py:122
  113.0 29.3 %copy-start.1 = (bf16[256,768]{1,0:T(8,128)(2,1)}, bf16[256,768]{1,0:T(8,128)(2,1)S(1)}, u32[]{:S(2)}) copy-start(bf16[256,768]{1,0:T(8,128)(2,1)S(1)} %fusion.4) | copy-start | bytes 1179652
  123.7 8.9 %all-to-all-start.6 = ((bf16[4,8,36]{2,0,1:T(4,128)(2,1)}), bf16[4,8,36]{2,0,1:T(4,128)(2,1)S(1)}, u32[]{:S(2)}, u32[]{:S(2)}) async-start(bf16[4,8,36]{2,0,1:T(4,128)(2,1)} %copy.159), calls=%async_computation.6 | async-start | bytes 16384 | tf_op jit(solution)/shard_map/all_to_all | solution.py:130
  133.2 9.3 %all-to-all-start.7 = ((bf16[4,2,144]{2,1,0:T(2,128)(2,1)}), bf16[4,2,144]{2,1,0:T(2,128)(2,1)S(1)}, u32[]{:S(2)}, u32[]{:S(2)}) async-start(bf16[4,2,144]{2,1,0:T(2,128)(2,1)} %reshape.370), calls=%async_computation.7 | async-start | bytes 8192 | tf_op jit(solution)/shard_map/all_to_all | solution.py:129
  136.5 9.6 %copy-start.3 = (f32[8]{0:T(128)S(1)}, f32[8]{0:T(128)}, u32[]{:S(2)}) copy-start(f32[8]{0:T(128)} %multiply_reduce_fusion.3) | copy-start | bytes 100
Sparse Core Ops, SparseCore 0:
  24.8 23.5 all-gather.1
